TPU v7x, 256 devices: a whole 4x4x8 slice. The times are simulated.
256 devices in a mesh: expert: 32 (over y, x, core), tensor: 8 (over z).
Axes of the slice: x: 4, y: 4, z: 8, core: 2. Of those that a mesh axis runs over, the one named last changes fastest.
Arguments:
- tokens: bfloat16 [16384, 4096], P('expert', 'tensor'), may hold values from -36 to 36
- expert_ids: int32 [16384, 1], P('expert'), may hold values from 0 to 63; in each aligned block of 512 rows (0 to 511, 512 to 1023, ...) at most 16 rows name the same one
- gates: float32 [16384, 1], P('expert'), may hold values from 0.25 to 1
- expert_in: bfloat16 [64, 4096, 2048], P('expert', 'tensor'), may hold values from -0.09375 to 0.09375
- expert_out: bfloat16 [64, 2048, 4096], P('expert', None, 'tensor'), may hold values from -0.125 to 0.125
- norm_gain: float32 [4096], replicated, may hold values from 0.5 to 2
- up_weight: bfloat16 [4096, 8192], P('expert', 'tensor'), may hold values from -0.09375 to 0.09375
- down_weight: bfloat16 [4096, 8192], P('expert', 'tensor'), may hold values from -0.0625 to 0.0625
Outputs:
- layer_output: bfloat16 [16384, 4096], P('expert', 'tensor')
Inputs may be any that keep to these rules, and one draw needn't show every extreme that they name: `expert_ids`: among the 512 tokens of one block, at most 16 carry the same expert id; in some blocks one id is carried by exactly 16 tokens.
All inputs are finite; a program needn't handle non-finite values.
Results may differ from a plain program's by a relative error of at most 0.015.
Values may be sent and summed in bfloat16 or wider, within the bound.
No kernel may reach another device: no remote copies, remote signals or barrier semaphores. Data moves between devices by JAX's collectives and lax.ppermute only.
A program may use at most 128 MiB of HBM per device.

v0:
```python
import jax
import jax.numpy as jnp
from jax import lax
from jax.sharding import PartitionSpec as P

EXP_DEV = 2


def slot_table(expert_col, experts, capacity):
    expert = expert_col[:, 0]
    count = expert.shape[0]
    order = jnp.arange(count, dtype=jnp.int32)
    same = (expert[:, None] == expert[None, :]) & (order[None, :] < order[:, None])
    position = jnp.sum(same.astype(jnp.int32), axis=1)
    slot_index = expert * capacity + position
    selector = jnp.arange(experts * capacity, dtype=jnp.int32)[:, None] == slot_index[None, :]
    return selector.astype(jnp.bfloat16)


def trade(buffer):
    result = lax.all_to_all(buffer, "expert", split_axis=0, concat_axis=0, tiled=True)
    return result


def gather_rows(weight, combine, start_value):
    return combine(start_value, lax.all_gather(weight, "expert", axis=0, tiled=True), jnp.int32(0))


def shards(tokens, expert_ids, gates, expert_in, expert_out, norm_gain, up_weight, down_weight):
    token_count = tokens.shape[0]
    local_width = tokens.shape[1]
    groups = lax.axis_size("expert")
    experts = EXP_DEV * groups
    capacity = 2 * token_count // experts
    selector = slot_table(expert_ids, experts, capacity)
    outgoing = jnp.dot(selector, tokens, preferred_element_type=jnp.float32).astype(jnp.bfloat16)
    outgoing = outgoing.reshape(groups, EXP_DEV, capacity, local_width)
    arrived = trade(outgoing)
    partial_value = jnp.einsum(
        "sjcd,jdh->sjch", arrived, expert_in, preferred_element_type=jnp.float32
    )
    summed = lax.psum(partial_value.astype(jnp.bfloat16), "tensor").astype(jnp.float32)
    active = jax.nn.relu(summed).astype(jnp.bfloat16)
    produced = jnp.einsum(
        "sjch,jhd->sjcd", active, expert_out, preferred_element_type=jnp.float32
    ).astype(jnp.bfloat16)
    returned = trade(produced).reshape(experts * capacity, local_width)
    routed = lax.dot_general(
        selector, returned, (((0,), (0,)), ((), ())), preferred_element_type=jnp.float32
    )
    mixed = (tokens.astype(jnp.float32) + gates * routed).astype(jnp.bfloat16)
    whole = lax.all_gather(mixed, "tensor", axis=1, tiled=True)
    whole_f32 = whole.astype(jnp.float32)
    mean_square = jnp.mean(whole_f32 * whole_f32, axis=1, keepdims=True)
    normed = (whole_f32 * lax.rsqrt(mean_square + 1e-06) * norm_gain).astype(jnp.bfloat16)

    def add_up(carry, piece, start):
        return jnp.dot(normed, piece, preferred_element_type=jnp.float32)

    ffn_hidden = gather_rows(
        up_weight, add_up, jnp.zeros((token_count, up_weight.shape[1]), jnp.float32)
    )
    ffn_active = jax.nn.gelu(ffn_hidden, approximate=True).astype(jnp.bfloat16)

    def add_down(carry, piece, start):
        contribution = lax.dot_general(
            ffn_active, piece, (((1,), (1,)), ((), ())), preferred_element_type=jnp.float32
        )
        return contribution

    outputs = gather_rows(
        down_weight, add_down, jnp.zeros((token_count, whole.shape[1]), jnp.float32)
    )
    summed_out = lax.psum_scatter(
        outputs.astype(jnp.bfloat16), "tensor", scatter_dimension=1, tiled=True
    ).astype(jnp.float32)
    return (mixed.astype(jnp.float32) + summed_out).astype(jnp.bfloat16)


def solution(mesh):
    return jax.shard_map(
        shards,
        mesh=mesh,
        in_specs=(
            P("expert", "tensor"),
            P("expert", None),
            P("expert", None),
            P("expert", "tensor", None),
            P("expert", None, "tensor"),
            P(),
            P("expert", "tensor"),
            P("expert", "tensor"),
        ),
        out_specs=P("expert", "tensor"),
        check_vma=False,
    )
```

profile of v0, /device:TPU:1, one launch (start us, length us, event | category | flops | bytes accessed | tf_op | source)
XLA Modules:
  0.0 422.7 jit_solution(1282529528484603267)
XLA Ops:
  6.5 1.1 convert_reduce_fusion
  7.6 0.9 multiply_add_fusion
  8.5 1.8 fusion.24
  10.3 25.6 %all_to_all.10 = bf16[32,2,16,512]{3,2,1,0:T(8,128)(2,1)S(1)} all-to-all(bf16[32,2,16,512]{3,2,1,0:T(8,128)(2,1)S(1)} %bitcast.30), channel_id=1, replica_groups=mesh['expert'=32,'tensor'=8] {'expert'}, dimensions={0} | all-to-all | bytes 2097152 | tf_op jit(solution)/shard_map/all_to_all | solution.py:21
  35.8 4.3 %convert_bitcast_fusion = bf16[32,2,16,2048]{3,2,0,1:T(8,128)(2,1)} fusion(bf16[2,512,2048]{2,1,0:T(8,128)(2,1)S(1)} %copy-done.1, bf16[32,2,16,512]{3,2,1,0:T(8,128)(2,1)S(1)} %all_to_all.10), kind=kOutput, calls=%fused_computation.15 | convolution fusion | flops 2149580800 | bytes 9437184 | tf_op jit(solution)/shard_map/sjcd,jdh->sjch/dot_general | solution.py:39
  40.2 0.0 all-gather.4.cloned.1.call-start
  40.2 108.1 %all-reduce.2.cloned.1.call-done = bf16[32,2,16,2048]{3,2,0,1:T(8,128)(2,1)} async-done(((bf16[32,2,16,2048]{3,2,0,1:T(8,128)(2,1)}), bf16[32,2,16,2048]{3,2,0,1:T(8,128)(2,1)}) %all-reduce.2.cloned.1.call-update) | async-done | bytes 4194320 | tf_op jit(solution)/shard_map/psum | solution.py:42
  148.3 5.8 %fusion.30 = bf16[32,2,16,512]{3,2,0,1:T(8,128)(2,1)S(1)} fusion(bf16[2,2048,512]{2,1,0:T(8,128)(2,1)} %param.12, bf16[32,2,16,2048]{3,2,0,1:T(8,128)(2,1)} %all-reduce.2.cloned.1.call-done), kind=kOutput, calls=%fused_computation.30 | convolution fusion | flops 2154299392 | bytes 9437184 | tf_op jit(solution)/shard_map/sjch,jhd->sjcd/dot_general | solution.py:44
  154.1 0.1 copy.15
  154.2 24.6 %all_to_all.11 = bf16[32,2,16,512]{3,2,1,0:T(8,128)(2,1)S(1)} all-to-all(bf16[32,2,16,512]{3,2,1,0:T(8,128)(2,1)S(1)} %copy.15), channel_id=1, replica_groups=mesh['expert'=32,'tensor'=8] {'expert'}, dimensions={0} | all-to-all | bytes 2097152 | tf_op jit(solution)/shard_map/all_to_all | solution.py:21
  178.9 1.6 fusion.35
  180.5 0.0 all-gather.6.cloned.1.call-start
  180.5 0.7 all-gather.6.cloned.1.call-update
  181.2 0.0 all-gather.8.cloned.1.call-start
  181.2 0.5 all-gather.8.cloned.1.call-update
  181.8 0.2 reduce-scatter.2.cloned.1.call-start
  182.0 48.4 %all-gather.4.cloned.1.call-done = bf16[512,4096]{1,0:T(8,128)(2,1)} async-done(((bf16[512,512]{1,0:T(8,128)(2,1)}), bf16[512,4096]{1,0:T(8,128)(2,1)}) %all-gather.4.cloned.1.call-update) | async-done | bytes 4194320 | tf_op jit(solution)/shard_map/all_gather | solution.py:52
  230.4 3.1 fusion
  233.4 56.4 %all-gather.6.cloned.1.call-done = bf16[4096,1024]{1,0:T(8,128)(2,1)} async-done(((bf16[128,1024]{1,0:T(8,128)(2,1)}), bf16[4096,1024]{1,0:T(8,128)(2,1)}) %all-gather.6.cloned.1.call-update) | async-done | bytes 8388624 | tf_op jit(solution)/shard_map/all_gather | solution.py:26
  289.9 9.6 %fusion.21 = bf16[512,1024]{1,0:T(8,128)(2,1)S(1)} fusion(bf16[4096,1024]{1,0:T(8,128)(2,1)} %all-gather.6.cloned.1.call-done, bf16[512,4096]{1,0:T(8,128)(2,1)} %all-gather.4.cloned.1.call-done, f32[4096]{0:T(1024)S(1)} %copy-done.3, f32[512]{0:T(512)S(1)} %add_rsqrt_fusion), kind=kOutput, calls=%fused_computation.24 | convolution fusion | flops 4308074496 | bytes 13649920 | tf_op jit(solution)/shard_map/dot_general | solution.py:58
  299.5 50.4 %all-gather.8.cloned.1.call-done = bf16[4096,1024]{1,0:T(8,128)(2,1)} async-done(((bf16[128,1024]{1,0:T(8,128)(2,1)}), bf16[4096,1024]{1,0:T(8,128)(2,1)}) %all-gather.8.cloned.1.call-update) | async-done | bytes 8388624 | tf_op jit(solution)/shard_map/all_gather | solution.py:26
  349.9 9.6 %convolution_convert_fusion = bf16[512,4096]{1,0:T(8,128)(2,1)} fusion(bf16[512,1024]{1,0:T(8,128)(2,1)S(1)} %fusion.21, bf16[4096,1024]{1,0:T(8,128)(2,1)} %all-gather.8.cloned.1.call-done), kind=kOutput, calls=%fused_computation.6 | convolution fusion | flops 4297064448 | bytes 13631488 | tf_op jit(solution)/shard_map/dot_general | solution.py:66
  359.5 54.7 %reduce-scatter.2.cloned.1.call-done = bf16[512,512]{1,0:T(8,128)(2,1)} async-done(((bf16[512,4096]{1,0:T(8,128)(2,1)}), bf16[512,512]{1,0:T(8,128)(2,1)}) %reduce-scatter.2.cloned.1.call-update) | async-done | bytes 524304 | tf_op jit(solution)/shard_map/reduce_scatter | solution.py:74
  414.2 2.0 add_convert_fusion
  (15 shorter events, 0.1 us)
Async XLA Ops:
  6.5 141.8 %all-reduce.2.cloned.1.call-start = ((), (), s32[]{:S(2)}) async-start(), calls=%async_computation.3 | async-start | bytes 8388608 | tf_op jit(solution)/shard_map/psum | solution.py:42
  6.5 29.3 %copy-start.1 = (bf16[2,512,2048]{2,1,0:T(8,128)(2,1)S(1)}, bf16[2,512,2048]{2,1,0:T(8,128)(2,1)}, u32[]{:S(2)}) copy-start(bf16[2,512,2048]{2,1,0:T(8,128)(2,1)} %param.11) | copy-start | bytes 12582916
  40.2 190.2 %all-gather.4.cloned.1.call-start = ((), (), s32[]{:S(2)}) async-start(), calls=%async_computation.4 | async-start | bytes 4718592 | tf_op jit(solution)/shard_map/all_gather | solution.py:52
  154.1 24.7 %copy-start.2 = (bf16[512,512]{1,0:T(8,128)(2,1)S(1)}, bf16[512,512]{1,0:T(8,128)(2,1)}, u32[]{:S(2)}) copy-start(bf16[512,512]{1,0:T(8,128)(2,1)} %param.8) | copy-start | bytes 1572868
  154.1 24.7 %copy-start.4 = (f32[512,1]{0,1:T(1,128)S(1)}, f32[512,1]{0,1:T(1,128)}, u32[]{:S(2)}) copy-start(f32[512,1]{0,1:T(1,128)} %param.10) | copy-start | bytes 6148
  178.9 111.0 %copy-start.3 = (f32[4096]{0:T(1024)S(1)}, f32[4096]{0:T(1024)}, u32[]{:S(2)}) copy-start(f32[4096]{0:T(1024)} %param.13) | copy-start | bytes 49156
  180.5 109.4 %all-gather.6.cloned.1.call-start = ((), (), s32[]{:S(2)}) async-start(), calls=%async_computation.5 | async-start | bytes 8650752 | tf_op jit(solution)/shard_map/all_gather | solution.py:26
  181.2 168.7 %all-gather.8.cloned.1.call-start = ((), (), s32[]{:S(2)}) async-start(), calls=%async_computation.6 | async-start | bytes 8650752 | tf_op jit(solution)/shard_map/all_gather | solution.py:26
  181.8 232.5 %reduce-scatter.2.cloned.1.call-start = ((), (), s32[]{:S(2)}) async-start(), calls=%async_computation.7 | async-start | bytes 4718592 | tf_op jit(solution)/shard_map/reduce_scatter | solution.py:74
  359.5 54.8 %copy-start = (bf16[512,512]{1,0:T(8,128)(2,1)S(1)}, bf16[512,512]{1,0:T(8,128)(2,1)}, u32[]{:S(2)}) copy-start(bf16[512,512]{1,0:T(8,128)(2,1)} %fusion.35) | copy-start | bytes 1572868
Sparse Core Ops, SparseCore 0:
  40.3 107.9 all-reduce.1
  180.6 49.7 all-gather.3
  232.9 56.9 all-gather.5
  292.3 57.5 all-gather.7
  359.6 54.5 reduce-scatter.1
where the time goes:
time: 423 us
  waiting for transfers between devices  319 us (75%)
  blocking collectives  50.2 us (12%)
  matrix products  32.6 us (8%)
  between operations  13.2 us (3%)
  other arithmetic  7.03 us (2%)
    psum x1, waiting for transfers between devices, shards(): lax.psum(partial_value.astype(jnp.bfloat16), 'tensor').astype(jnp.float32)  108 us
    all_gather x2, waiting for transfers between devices, gather_rows(): lax.all_gather(weight, 'expert', axis=0, tiled=True)  107 us
    reduce_scatter x1, waiting for transfers between devices, shards(): lax.psum_scatter(outputs.astype(jnp.bfloat16), 'tensor', scatter_dimensio...  54.7 us
    all_to_all x2, blocking collectives, trade(): lax.all_to_all(buffer, 'expert', split_axis=0, concat_axis=0, tiled=True)  50.2 us
    all_gather x1, waiting for transfers between devices, shards(): whole = lax.all_gather(mixed, 'tensor', axis=1, tiled=True)  48.4 us
    dot_general x1, matrix products, add_up(): return jnp.dot(normed, piece, preferred_element_type=jnp.float32)  9.58 us
    dot_general x1, matrix products, add_down(): lax.dot_general(ffn_active, piece, (((1,), (1,)), ((), ())), preferred_el...  9.57 us
  transfers between devices with their start and end apart: 5, of which 5 were waited for; matrix products, arithmetic and copies ran while one was open for 3% of the time, Pallas kernels for 0%

commit v1 on v0

--- a/solution.py
+++ b/solution.py
@@ -49,7 +49,14 @@
         selector, returned, (((0,), (0,)), ((), ())), preferred_element_type=jnp.float32
     )
     mixed = (tokens.astype(jnp.float32) + gates * routed).astype(jnp.bfloat16)
-    whole = lax.all_gather(mixed, "tensor", axis=1, tiled=True)
+    size = lax.axis_size("tensor")
+    right = [(i, (i + 1) % size) for i in range(size)]
+    blocks = [mixed]
+    for hop in range(1, size):
+        blocks = [lax.ppermute(blocks[0], "tensor", right), *blocks]
+    result_2 = jnp.concatenate(blocks, axis=1)
+    shift = (lax.axis_index("tensor") + 1) * blocks[-1].shape[1]
+    whole = jnp.roll(result_2, shift, axis=1)
     whole_f32 = whole.astype(jnp.float32)
     mean_square = jnp.mean(whole_f32 * whole_f32, axis=1, keepdims=True)
     normed = (whole_f32 * lax.rsqrt(mean_square + 1e-06) * norm_gain).astype(jnp.bfloat16)

time: 423 us -> 366 us (0.87)
  waiting for transfers between devices: 319 us -> 269 us
  blocking collectives: 50.2 us -> 25.6 us
  local copies, waits for them, and re-layouts: 0.09 us -> 10.2 us
  starting transfers between devices: 0.34 us -> 7.76 us
    all_gather x2, waiting for transfers between devices: 107 us -> 0.05 us  [gather_rows(): lax.all_gather(weight, 'expert', axis=0, tiled=True)]
    ppermute x0 -> x7, waiting for transfers between devices: none -> 83.5 us  [shards(): blocks = [lax.ppermute(blocks[0], 'tensor', right), *blocks]]
    all_gather x1 -> x0, waiting for transfers between devices: 48.4 us -> none  [shards(): whole = lax.all_gather(mixed, 'tensor', axis=1, tiled=True)]
    all_to_all x2 -> x1, blocking collectives: 50.2 us -> 25.6 us  [trade(): lax.all_to_all(buffer, 'expert', split_axis=0, concat_axis=0, tiled=True)]
    all_to_all x0 -> x1, waiting for transfers between devices: none -> 16.9 us  [trade(): lax.all_to_all(buffer, 'expert', split_axis=0, concat_axis=0, tiled=True)]
    unnamed x10 -> x24, local copies, waits for them, and re-layouts: 0.02 us -> 8.16 us
    all_to_all x0 -> x1, starting transfers between devices: none -> 7.54 us  [trade(): lax.all_to_all(buffer, 'expert', split_axis=0, concat_axis=0, tiled=True)]
    reduce_scatter x1, waiting for transfers between devices: 54.7 us -> 60.2 us  [shards(): lax.psum_scatter(outputs.astype(jnp.bfloat16), 'tensor', scatter_dimensio...]
  transfers between devices with their start and end apart: 5 -> 12, of which waited for: 5 -> 10; matrix products, arithmetic and copies ran while one was open for 3% -> 6% of each run, Pallas kernels for 0% -> 0%
where the time goes in v1:
time: 366 us
  waiting for transfers between devices  269 us (73%)
  matrix products  34.4 us (9%)
  blocking collectives  25.6 us (7%)
  between operations  15.1 us (4%)
  local copies, waits for them, and re-layouts  10.2 us (3%)
  starting transfers between devices  7.76 us (2%)
  other arithmetic  3.82 us (1%)
    psum x1, waiting for transfers between devices, shards(): lax.psum(partial_value.astype(jnp.bfloat16), 'tensor').astype(jnp.float32)  107 us
    ppermute x7, waiting for transfers between devices, shards(): blocks = [lax.ppermute(blocks[0], 'tensor', right), *blocks]  83.5 us
    reduce_scatter x1, waiting for transfers between devices, shards(): lax.psum_scatter(outputs.astype(jnp.bfloat16), 'tensor', scatter_dimensio...  60.2 us
    all_to_all x1, blocking collectives, trade(): lax.all_to_all(buffer, 'expert', split_axis=0, concat_axis=0, tiled=True)  25.6 us
    all_to_all x1, waiting for transfers between devices, trade(): lax.all_to_all(buffer, 'expert', split_axis=0, concat_axis=0, tiled=True)  16.9 us
    dot_general x1, matrix products, add_up(): return jnp.dot(normed, piece, preferred_element_type=jnp.float32)  9.65 us
    dot_general x1, matrix products, add_down(): lax.dot_general(ffn_active, piece, (((1,), (1,)), ((), ())), preferred_el...  9.55 us
    unnamed x24, local copies, waits for them, and re-layouts  8.16 us
  transfers between devices with their start and end apart: 12, of which 10 were waited for; matrix products, arithmetic and copies ran while one was open for 6% of the time, Pallas kernels for 0%

profile of v1, /device:TPU:1, one launch (start us, length us, event | category | flops | bytes accessed | tf_op | source)
XLA Modules:
  0.0 365.6 jit_solution(17387874426519163362)
XLA Ops:
  9.1 1.8 fusion.27
  10.8 25.6 %all_to_all.10 = bf16[32,2,16,512]{3,2,1,0:T(8,128)(2,1)S(1)} all-to-all(bf16[32,2,16,512]{3,2,1,0:T(8,128)(2,1)S(1)} %bitcast.30), channel_id=1, replica_groups=mesh['expert'=32,'tensor'=8] {'expert'}, dimensions={0} | all-to-all | bytes 2097152 | tf_op jit(solution)/shard_map/all_to_all | solution.py:21
  36.4 6.6 %convert_bitcast_fusion = bf16[32,2,16,2048]{3,2,0,1:T(8,128)(2,1)} fusion(bf16[2,512,2048]{2,1,0:T(8,128)(2,1)} %param.11, bf16[32,2,16,512]{3,2,1,0:T(8,128)(2,1)S(1)} %all_to_all.10), kind=kOutput, calls=%fused_computation.15 | convolution fusion | flops 2149580800 | bytes 9437184 | tf_op jit(solution)/shard_map/sjcd,jdh->sjch/dot_general | solution.py:39
  44.2 106.9 %all-reduce.2.cloned.1.call-done = bf16[32,2,16,2048]{3,2,0,1:T(8,128)(2,1)} async-done(((bf16[32,2,16,2048]{3,2,0,1:T(8,128)(2,1)}), bf16[32,2,16,2048]{3,2,0,1:T(8,128)(2,1)}) %all-reduce.2.cloned.1.call-update) | async-done | bytes 4194320 | tf_op jit(solution)/shard_map/psum | solution.py:42
  151.1 6.1 %fusion.31 = bf16[32,2,16,512]{3,2,0,1:T(8,128)(2,1)S(1)} fusion(bf16[2,2048,512]{2,1,0:T(8,128)(2,1)} %param.12, bf16[32,2,16,2048]{3,2,0,1:T(8,128)(2,1)} %all-reduce.2.cloned.1.call-done), kind=kOutput, calls=%fused_computation.31 | convolution fusion | flops 2154299392 | bytes 9437184 | tf_op jit(solution)/shard_map/sjch,jhd->sjcd/dot_general | solution.py:44
  157.2 1.0 copy.28
  158.3 7.5 %all-to-all-start.1 = ((bf16[32,2,16,512]{3,2,1,0:T(8,128)(2,1)}), bf16[32,2,16,512]{3,2,1,0:T(8,128)(2,1)S(1)}, u32[]{:S(2)}, u32[]{:S(2)}) async-start(bf16[32,2,16,512]{3,2,1,0:T(8,128)(2,1)} %copy.28), calls=%async_computation.1 | async-start | bytes 2097152 | tf_op jit(solution)/shard_map/all_to_all | solution.py:21
  166.1 16.9 %all-to-all-done.1 = bf16[32,2,16,512]{3,2,1,0:T(8,128)(2,1)S(1)} async-done(((bf16[32,2,16,512]{3,2,1,0:T(8,128)(2,1)}), bf16[32,2,16,512]{3,2,1,0:T(8,128)(2,1)S(1)}, u32[]{:S(2)}, u32[]{:S(2)}) %all-to-all-start.1) | async-done | bytes 1048608 | tf_op jit(solution)/shard_map/all_to_all | solution.py:21
  183.9 14.3 %collective-permute-done = bf16[512,512]{0,1:T(8,128)(2,1)S(1)} collective-permute-done((bf16[512,512]{0,1:T(8,128)(2,1)S(1)}, bf16[512,512]{0,1:T(8,128)(2,1)S(1)}, u32[]{:S(2)}, u32[]{:S(2)}) %collective-permute-start) | collective-permute-done | bytes 524320 | tf_op jit(solution)/shard_map/ppermute | solution.py:56
  198.2 13.4 %collective-permute-done.1 = bf16[512,512]{0,1:T(8,128)(2,1)S(1)} collective-permute-done((bf16[512,512]{0,1:T(8,128)(2,1)S(1)}, bf16[512,512]{0,1:T(8,128)(2,1)S(1)}, u32[]{:S(2)}, u32[]{:S(2)}) %collective-permute-start.1) | collective-permute-done | bytes 524320 | tf_op jit(solution)/shard_map/ppermute | solution.py:56
  211.6 12.5 %collective-permute-done.2 = bf16[512,512]{0,1:T(8,128)(2,1)S(1)} collective-permute-done((bf16[512,512]{0,1:T(8,128)(2,1)S(1)}, bf16[512,512]{0,1:T(8,128)(2,1)S(1)}, u32[]{:S(2)}, u32[]{:S(2)}) %collective-permute-start.2) | collective-permute-done | bytes 524320 | tf_op jit(solution)/shard_map/ppermute | solution.py:56
  224.1 11.6 %collective-permute-done.3 = bf16[512,512]{0,1:T(8,128)(2,1)S(1)} collective-permute-done((bf16[512,512]{0,1:T(8,128)(2,1)S(1)}, bf16[512,512]{0,1:T(8,128)(2,1)S(1)}, u32[]{:S(2)}, u32[]{:S(2)}) %collective-permute-start.3) | collective-permute-done | bytes 524320 | tf_op jit(solution)/shard_map/ppermute | solution.py:56
  235.6 10.6 %collective-permute-done.4 = bf16[512,512]{0,1:T(8,128)(2,1)S(1)} collective-permute-done((bf16[512,512]{0,1:T(8,128)(2,1)S(1)}, bf16[512,512]{0,1:T(8,128)(2,1)S(1)}, u32[]{:S(2)}, u32[]{:S(2)}) %collective-permute-start.4) | collective-permute-done | bytes 524320 | tf_op jit(solution)/shard_map/ppermute | solution.py:56
  246.3 10.5 %collective-permute-done.5 = bf16[512,512]{0,1:T(8,128)(2,1)} collective-permute-done((bf16[512,512]{0,1:T(8,128)(2,1)S(1)}, bf16[512,512]{0,1:T(8,128)(2,1)}, u32[]{:S(2)}, u32[]{:S(2)}) %collective-permute-start.5) | collective-permute-done | bytes 524320 | tf_op jit(solution)/shard_map/ppermute | solution.py:56
  256.8 10.7 %collective-permute-done.6 = bf16[512,512]{0,1:T(8,128)(2,1)} collective-permute-done((bf16[512,512]{0,1:T(8,128)(2,1)}, bf16[512,512]{0,1:T(8,128)(2,1)}, u32[]{:S(2)}, u32[]{:S(2)}) %collective-permute-start.6) | collective-permute-done | bytes 524320 | tf_op jit(solution)/shard_map/ppermute | solution.py:56
  267.4 1.1 constant_dynamic-update-slice_fusion.15
  268.5 1.1 constant_dynamic-update-slice_fusion.14
  269.9 1.1 constant_dynamic-update-slice_fusion.7
  271.0 1.1 constant_dynamic-update-slice_fusion.6
  272.3 3.2 copy-done
  276.5 9.6 %fusion.22 = bf16[512,1024]{1,0:T(8,128)(2,1)S(1)} fusion(bf16[4096,1024]{1,0:T(8,128)(2,1)} %all-gather.3.cloned.1.call-done, f32[4096]{0:T(1024)S(1)} %copy-done.2, f32[512]{0:T(512)S(1)} %add_rsqrt_fusion, bf16[512,8192]{0,1:T(8,128)(2,1)} %copy-done, s32[]{:T(128)S(6)} %select_n.14), kind=kOutput, calls=%fused_computation.25 | convolution fusion | flops 4308074496 | bytes 13649924 | tf_op jit(solution)/shard_map/dot_general | solution.py:65
  286.2 9.5 %convolution_convert_fusion = bf16[512,4096]{0,1:T(8,128)(2,1)} fusion(bf16[512,1024]{1,0:T(8,128)(2,1)S(1)} %fusion.22, bf16[4096,1024]{1,0:T(8,128)(2,1)} %all-gather.5.cloned.1.call-done), kind=kOutput, calls=%fused_computation.6 | convolution fusion | flops 4297064448 | bytes 13631488 | tf_op jit(solution)/shard_map/dot_general | solution.py:73
  295.8 60.2 %reduce-scatter.2.cloned.1.call-done = bf16[512,512]{0,1:T(8,128)(2,1)} async-done(((bf16[512,4096]{0,1:T(8,128)(2,1)}), bf16[512,512]{0,1:T(8,128)(2,1)}) %reduce-scatter.2.cloned.1.call-update) | async-done | bytes 524304 | tf_op jit(solution)/shard_map/reduce_scatter | solution.py:81
  356.0 1.2 add_convert_fusion
  (43 shorter events, 6.5 us)
Async XLA Ops:
  7.4 143.7 %all-reduce.2.cloned.1.call-start = ((), (), s32[]{:S(2)}) async-start(), calls=%async_computation.3 | async-start | bytes 8388608 | tf_op jit(solution)/shard_map/psum | solution.py:42
  43.0 233.5 %all-gather.3.cloned.1.call-start = ((), (), s32[]{:S(2)}) async-start(), calls=%async_computation.4 | async-start | bytes 8650752 | tf_op jit(solution)/shard_map/all_gather | solution.py:26
  43.6 242.6 %all-gather.5.cloned.1.call-start = ((), (), s32[]{:S(2)}) async-start(), calls=%async_computation.5 | async-start | bytes 8650752 | tf_op jit(solution)/shard_map/all_gather | solution.py:26
  44.2 121.7 %copy-start.1 = (bf16[512,512]{1,0:T(8,128)(2,1)S(1)}, bf16[512,512]{1,0:T(8,128)(2,1)}, u32[]{:S(2)}) copy-start(bf16[512,512]{1,0:T(8,128)(2,1)} %param.8) | copy-start | bytes 1572868
  44.2 138.8 %copy-start.3 = (f32[512,1]{0,1:T(1,128)S(1)}, f32[512,1]{0,1:T(1,128)}, u32[]{:S(2)}) copy-start(f32[512,1]{0,1:T(1,128)} %param.10) | copy-start | bytes 6148
  158.3 24.7 %all-to-all-start.1 = ((bf16[32,2,16,512]{3,2,1,0:T(8,128)(2,1)}), bf16[32,2,16,512]{3,2,1,0:T(8,128)(2,1)S(1)}, u32[]{:S(2)}, u32[]{:S(2)}) async-start(bf16[32,2,16,512]{3,2,1,0:T(8,128)(2,1)} %copy.28), calls=%async_computation.1 | async-start | bytes 2097152 | tf_op jit(solution)/shard_map/all_to_all | solution.py:21
  165.8 190.2 %reduce-scatter.2.cloned.1.call-start = ((), (), s32[]{:S(2)}) async-start(), calls=%async_computation.6 | async-start | bytes 4718592 | tf_op jit(solution)/shard_map/reduce_scatter | solution.py:81
  183.8 14.4 %collective-permute-start = (bf16[512,512]{0,1:T(8,128)(2,1)S(1)}, bf16[512,512]{0,1:T(8,128)(2,1)S(1)}, u32[]{:S(2)}, u32[]{:S(2)}) collective-permute-start(bf16[512,512]{0,1:T(8,128)(2,1)S(1)} %fusion.36), channel_id=1, source_target_pairs={{0,1},{1,2},{2,3},{3,4},{4,5},{5,6},{6,7},{7,0},{8,9},{9,10},{10,1... | collective-permute-start | bytes 1572872 | tf_op jit(solution)/shard_map/ppermute | solution.py:56
  198.2 13.4 %collective-permute-start.1 = (bf16[512,512]{0,1:T(8,128)(2,1)S(1)}, bf16[512,512]{0,1:T(8,128)(2,1)S(1)}, u32[]{:S(2)}, u32[]{:S(2)}) collective-permute-start(bf16[512,512]{0,1:T(8,128)(2,1)S(1)} %collective-permute-done), channel_id=1, source_target_pairs={{0,1},{1,2},{2,3},{3,4},{4,5},{5,6},{6,7},{7,0},{8,9},{9,10},{10,1... | collective-permute-start | bytes 1572872 | tf_op jit(solution)/shard_map/ppermute | solution.py:56
  211.6 12.5 %collective-permute-start.2 = (bf16[512,512]{0,1:T(8,128)(2,1)S(1)}, bf16[512,512]{0,1:T(8,128)(2,1)S(1)}, u32[]{:S(2)}, u32[]{:S(2)}) collective-permute-start(bf16[512,512]{0,1:T(8,128)(2,1)S(1)} %collective-permute-done.1), channel_id=1, source_target_pairs={{0,1},{1,2},{2,3},{3,4},{4,5},{5,6},{6,7},{7,0},{8,9},{9,10},{10,1... | collective-permute-start | bytes 1572872 | tf_op jit(solution)/shard_map/ppermute | solution.py:56
  224.1 11.6 %collective-permute-start.3 = (bf16[512,512]{0,1:T(8,128)(2,1)S(1)}, bf16[512,512]{0,1:T(8,128)(2,1)S(1)}, u32[]{:S(2)}, u32[]{:S(2)}) collective-permute-start(bf16[512,512]{0,1:T(8,128)(2,1)S(1)} %collective-permute-done.2), channel_id=1, source_target_pairs={{0,1},{1,2},{2,3},{3,4},{4,5},{5,6},{6,7},{7,0},{8,9},{9,10},{10,1... | collective-permute-start | bytes 1572872 | tf_op jit(solution)/shard_map/ppermute | solution.py:56
  235.6 10.6 %collective-permute-start.4 = (bf16[512,512]{0,1:T(8,128)(2,1)S(1)}, bf16[512,512]{0,1:T(8,128)(2,1)S(1)}, u32[]{:S(2)}, u32[]{:S(2)}) collective-permute-start(bf16[512,512]{0,1:T(8,128)(2,1)S(1)} %collective-permute-done.3), channel_id=1, source_target_pairs={{0,1},{1,2},{2,3},{3,4},{4,5},{5,6},{6,7},{7,0},{8,9},{9,10},{10,1... | collective-permute-start | bytes 1572872 | tf_op jit(solution)/shard_map/ppermute | solution.py:56
  246.3 10.5 %collective-permute-start.5 = (bf16[512,512]{0,1:T(8,128)(2,1)S(1)}, bf16[512,512]{0,1:T(8,128)(2,1)}, u32[]{:S(2)}, u32[]{:S(2)}) collective-permute-start(bf16[512,512]{0,1:T(8,128)(2,1)S(1)} %collective-permute-done.4), channel_id=1, source_target_pairs={{0,1},{1,2},{2,3},{3,4},{4,5},{5,6},{6,7},{7,0},{8,9},{9,10},{10,1... | collective-permute-start | bytes 1572872 | tf_op jit(solution)/shard_map/ppermute | solution.py:56
  256.7 10.7 %collective-permute-start.6 = (bf16[512,512]{0,1:T(8,128)(2,1)}, bf16[512,512]{0,1:T(8,128)(2,1)}, u32[]{:S(2)}, u32[]{:S(2)}) collective-permute-start(bf16[512,512]{0,1:T(8,128)(2,1)} %collective-permute-done.5), channel_id=1, source_target_pairs={{0,1},{1,2},{2,3},{3,4},{4,5},{5,6},{6,7},{7,0},{8,9},{9,10},{10,1... | collective-permute-start | bytes 1572872 | tf_op jit(solution)/shard_map/ppermute | solution.py:56
  269.7 6.8 %copy-start.2 = (f32[4096]{0:T(1024)S(1)}, f32[4096]{0:T(1024)}, u32[]{:S(2)}) copy-start(f32[4096]{0:T(1024)} %param.13) | copy-start | bytes 49156
  272.3 3.2 copy-start
Sparse Core Ops, SparseCore 0:
  43.1 107.9 all-reduce.1
  295.9 60.0 reduce-scatter.1
Sparse Core Ops, SparseCore 1:
  46.0 57.1 all-gather.2
  105.6 57.4 all-gather.4
